TPU v7x, 512 devices: a whole 4x4x16 slice. The times are simulated.
512 devices in a mesh: context: 32 (over z, core), fheads: 4 (over x), seqs: 4 (over y).
Axes of the slice: x: 4, y: 4, z: 16, core: 2. Of those that a mesh axis runs over, the one named last changes fastest.
Arguments:
- query_rows: bfloat16 [65536, 3072], P(('seqs', 'context'), 'fheads'), parts along dimension 0, may hold values from -5 to 5
- key_rows: bfloat16 [65536, 3072], P(('seqs', 'context'), 'fheads'), parts along dimension 0, may hold values from -5 to 5
- value_rows: bfloat16 [65536, 3072], P(('seqs', 'context'), 'fheads'), parts along dimension 0, may hold values from -10 to 10
- step_sizes: float32 [65536, 4], P(('seqs', 'context'), 'fheads'), parts along dimension 0, may hold values from 2e-05 to 0.0018
- w_gate: bfloat16 [4, 768, 768], P('fheads', 'context'), may hold values from -4 to 4
- w_up: bfloat16 [4, 768, 768], P('fheads', 'context'), may hold values from -4 to 4
- w_down: bfloat16 [4, 768, 768], P('fheads', 'context'), may hold values from -4 to 4
Outputs:
- window_out: bfloat16 [65536, 3072], P(('seqs', 'context'), 'fheads'), parts along dimension 0
- fast_out: bfloat16 [65536, 3072], P(('seqs', 'context'), 'fheads'), parts along dimension 0
There are 4 independent parts, one for each index of `seqs`. A program takes and returns all parts, laid end to end along the dimension named above; an argument that names none is the same for every part. Nothing has to cross between parts.
All inputs are finite; a program needn't handle non-finite values.
Results may differ from a plain program's by a relative error of at most 0.035.
Values may be sent and summed in bfloat16 or wider, within the bound.
A program may use at most 128 MiB of HBM per device.

v0:
```python
import math

import jax
import jax.numpy as jnp
from jax import lax
from jax.sharding import PartitionSpec as P

HD = 128
WINDOW = 512


def passed_along(x, axis, by):
    peers = lax.axis_size(axis)
    pairs = [(i, i + by) for i in range(peers) if 0 <= i + by < peers]
    return lax.ppermute(x, axis, pairs)


def unit_rows(values):
    return values * lax.rsqrt(jnp.mean(values * values, axis=-1, keepdims=True) + 1e-06)


def window_block(queries, keys_near, values_near, first_pos):
    row_count = queries.shape[0]
    query_pos = first_pos + jnp.arange(row_count, dtype=jnp.int32)
    key_pos = first_pos - WINDOW + jnp.arange(row_count + WINDOW, dtype=jnp.int32)
    allowed = (
        (key_pos[None, :] >= 0)
        & (key_pos[None, :] <= query_pos[:, None])
        & (key_pos[None, :] > query_pos[:, None] - WINDOW)
    )
    scores = jnp.einsum(
        "ihd,jhd->hij", queries, keys_near, preferred_element_type=jnp.float32
    ) / math.sqrt(HD)
    scores = jnp.where(allowed[None], scores, -1e30)
    row_max = jnp.max(scores, axis=-1, keepdims=True)
    powers = jnp.exp(scores - row_max)
    weights = (powers / jnp.sum(powers, axis=-1, keepdims=True)).astype(jnp.bfloat16)
    attended = jnp.einsum("hij,jhd->ihd", weights, values_near, preferred_element_type=jnp.float32)
    return attended.astype(jnp.bfloat16)


def dot_rows(first_op, second_op):
    return lax.dot_general(
        first_op, second_op, (((0,), (0,)), ((), ())), preferred_element_type=jnp.float32
    )


def dot_back(first_op, second_op):
    return lax.dot_general(
        first_op, second_op, (((1,), (1,)), ((), ())), preferred_element_type=jnp.float32
    )


def renormed(weight, gradient):
    initial = weight.astype(jnp.float32)
    fresh_rows = initial - gradient
    old_ms = jnp.mean(initial * initial, axis=0)
    new_ms = jnp.mean(fresh_rows * fresh_rows, axis=0)
    return (fresh_rows * jnp.sqrt(old_ms) * lax.rsqrt(new_ms + 1e-06)).astype(jnp.bfloat16)


def apply_fast(fast_queries, gate_w, up_w, down_w):
    gate_new = jnp.dot(fast_queries, gate_w, preferred_element_type=jnp.float32)
    up_new = jnp.dot(fast_queries, up_w, preferred_element_type=jnp.float32)
    hidden_new = (gate_new * jax.nn.sigmoid(gate_new) * up_new).astype(jnp.bfloat16)
    return jnp.dot(hidden_new, down_w, preferred_element_type=jnp.float32).astype(jnp.bfloat16)


def body(query_rows, key_rows, value_rows, step_sizes, w_gate, w_up, w_down):
    row_count = query_rows.shape[0]
    heads_here = query_rows.shape[1] // HD
    rim_keys, rim_values = passed_along((key_rows, value_rows), "context", 1)
    first_pos = lax.axis_index("context") * row_count
    keys_near = jnp.concatenate([rim_keys, key_rows], axis=0).reshape(
        row_count + WINDOW, heads_here, HD
    )
    values_near = jnp.concatenate([rim_values, value_rows], axis=0).reshape(
        row_count + WINDOW, heads_here, HD
    )
    window_out = window_block(
        query_rows.reshape(row_count, heads_here, HD), keys_near, values_near, first_pos
    )
    window_out = window_out.reshape(row_count, heads_here * HD)
    gathered = (
        lax.all_gather(w_gate, "context", axis=1, tiled=True),
        lax.all_gather(w_up, "context", axis=1, tiled=True),
        lax.all_gather(w_down, "context", axis=1, tiled=True),
    )
    gate_w = gathered[0][0]
    up_w = gathered[1][0]
    down_w = gathered[2][0]
    fast_keys = unit_rows(key_rows.astype(jnp.float32)).astype(jnp.bfloat16)
    fast_queries = unit_rows(query_rows.astype(jnp.float32)).astype(jnp.bfloat16)
    target = (-(step_sizes * value_rows.astype(jnp.float32))).astype(jnp.bfloat16)
    gate_pre = jnp.dot(fast_keys, gate_w, preferred_element_type=jnp.float32)
    up_pre = jnp.dot(fast_keys, up_w, preferred_element_type=jnp.float32)
    sigmoid_gate = jax.nn.sigmoid(gate_pre)
    hidden = (gate_pre * sigmoid_gate * up_pre).astype(jnp.bfloat16)
    back_grad = dot_back(target, down_w)
    d_gate = (back_grad * up_pre * sigmoid_gate * (1.0 + gate_pre * (1.0 - sigmoid_gate))).astype(
        jnp.bfloat16
    )
    d_up = (back_grad * gate_pre * sigmoid_gate).astype(jnp.bfloat16)
    grad_gate = dot_rows(fast_keys, d_gate)
    grad_up = dot_rows(fast_keys, d_up)
    grad_down = dot_rows(hidden, target)
    summed = (
        lax.psum(grad_gate.astype(jnp.bfloat16), "context").astype(jnp.float32),
        lax.psum(grad_up.astype(jnp.bfloat16), "context").astype(jnp.float32),
        lax.psum(grad_down.astype(jnp.bfloat16), "context").astype(jnp.float32),
    )
    updated_gate = renormed(gate_w, summed[0])
    updated_up = renormed(up_w, summed[1])
    updated_down = renormed(down_w, summed[2])
    fast_out = apply_fast(fast_queries, updated_gate, updated_up, updated_down)
    return (window_out, fast_out)


def solution(mesh):
    in_specs = (
        P(("seqs", "context"), "fheads"),
        P(("seqs", "context"), "fheads"),
        P(("seqs", "context"), "fheads"),
        P(("seqs", "context"), "fheads"),
        P("fheads", "context", None),
        P("fheads", "context", None),
        P("fheads", "context", None),
    )
    out_specs = (P(("seqs", "context"), "fheads"), P(("seqs", "context"), "fheads"))
    return jax.shard_map(body, mesh=mesh, in_specs=in_specs, out_specs=out_specs, check_vma=False)
```

profile of v0, /device:TPU:1, one launch (start us, length us, event | category | flops | bytes accessed | tf_op | source)
XLA Modules:
  0.0 467.8 jit_solution(14583098980945842931)
XLA Ops:
  7.2 0.0 copy-start
  7.2 0.0 copy-start.1
  7.2 0.0 all-gather.4.cloned.1.call-start
  7.2 0.7 all-gather.4.cloned.1.call-update
  7.9 0.0 all-gather.8.cloned.1.call-start
  8.0 0.7 all-gather.8.cloned.1.call-update
  8.7 0.0 all-gather.6.cloned.1.call-start
  8.7 1.4 copy.14
  10.1 4.9 %collective-permute-start.1 = (bf16[512,768]{0,1:T(8,128)(2,1)S(1)}, bf16[512,768]{0,1:T(8,128)(2,1)}, u32[]{:S(2)}, u32[]{:S(2)}) collective-permute-start(bf16[512,768]{0,1:T(8,128)(2,1)S(1)} %copy.14), channel_id=1, source_target_pairs={{0,16},{16,32},{32,48},{48,64},{64,80},{80,96},{96,112},{112,128},... | collective-permute-start | bytes 2359304 | tf_op jit(solution)/shard_map/ppermute | solution.py:15
  15.1 1.9 collective-permute-start
  17.0 0.0 all-gather.6.cloned.1.call-update
  17.0 0.0 all-reduce.3.cloned.1.call-start
  17.1 0.0 copy-done
  17.1 0.2 fusion.11
  17.3 0.0 copy-done.1
  17.3 0.2 fusion.9
  17.6 0.3 copy.16
  17.9 1.6 compare_and_fusion
  19.5 4.5 collective-permute-done.1
  24.0 2.6 pad_maximum_fusion.1
  26.6 11.0 %fusion.45 = (f32[6,512]{1,0:T(8,128)S(1)}, f32[6,512,1024]{1,2,0:T(8,128)}) fusion(pred[512,1024]{0,1:T(8,128)(4,1)} %compare_and_fusion, bf16[1024,6,128]{0,2,1:T(8,128)(2,1)} %bitcast.52, bf16[512,6,128]{0,2,1:T(8,128)(2,1)S(1)} %bitcast.54), kind=kOutput, calls=%fused_computation.81 | convolution fusion | flops 817890304 | bytes 15478784 | tf_op jit(solution)/shard_map/sub | solution.py:36
  37.6 49.4 %all-gather.4.cloned.1.call-done = bf16[1,768,768]{2,1,0:T(8,128)(2,1)} async-done(((bf16[1,24,768]{2,1,0:T(8,128)(2,1)}), bf16[1,768,768]{2,1,0:T(8,128)(2,1)}) %all-gather.4.cloned.1.call-update) | async-done | bytes 1179664 | tf_op jit(solution)/shard_map/all_gather | solution.py:85
  86.9 2.1 fusion.21
  89.0 0.0 copy-start.6
  89.0 68.2 %all-gather.8.cloned.1.call-done = bf16[1,768,768]{2,1,0:T(8,128)(2,1)} async-done(((bf16[1,24,768]{2,1,0:T(8,128)(2,1)}), bf16[1,768,768]{2,1,0:T(8,128)(2,1)}) %all-gather.8.cloned.1.call-update) | async-done | bytes 1179664 | tf_op jit(solution)/shard_map/all_gather | solution.py:86
  157.2 2.1 fusion.16
  159.3 0.0 copy-start.7
  159.3 1.2 copy-done.7
  160.5 0.0 copy-done.6
  160.5 3.2 convolution_convert_fusion
  163.7 63.7 %all-gather.6.cloned.1.call-done = bf16[1,768,768]{2,1,0:T(8,128)(2,1)} async-done(((bf16[1,24,768]{2,1,0:T(8,128)(2,1)}), bf16[1,768,768]{2,1,0:T(8,128)(2,1)}) %all-gather.6.cloned.1.call-update) | async-done | bytes 1179664 | tf_op jit(solution)/shard_map/all_gather | solution.py:87
  227.5 2.3 fusion.19
  229.8 0.0 copy-start.8
  229.8 2.0 convolution_convert_fusion.1
  231.9 2.2 convolution_convert_fusion.2
  234.1 0.0 all-reduce.3.cloned.1.call-update
  234.1 0.0 collective-permute-done
  234.1 1.5 pad_maximum_fusion
  235.6 1.7 copy.13
  237.3 6.1 %fusion.13 = bf16[6,128,512]{2,1,0:T(8,128)(2,1)S(1)} fusion(bf16[1024,6,128]{0,2,1:T(8,128)(2,1)} %bitcast.53, f32[6,512,1024]{1,2,0:T(8,128)} %get-tuple-element.16, f32[6,512]{1,0:T(8,128)S(1)} %get-tuple-element.15), kind=kOutput, calls=%fused_computation.45 | convolution fusion | flops 811991040 | bytes 14954496 | tf_op jit(solution)/shard_map/hij,jhd->ihd/dot_general | solution.py:38
  243.3 1.2 copy.20
  244.5 204.4 %all-reduce.3.cloned.1.call-done = (bf16[768,768]{1,0:T(8,128)(2,1)}, bf16[768,768]{1,0:T(8,128)(2,1)}, bf16[768,768]{1,0:T(8,128)(2,1)}) async-done(((bf16[768,768]{1,0:T(8,128)(2,1)}, bf16[768,768]{1,0:T(8,128)(2,1)}, bf16[768,768]{1,0:T(8,128)(2,1)}), (bf16[768,768]{1,0:T(8,128)(2,1)}, bf16[768,768]{1,0:T(8,128)(2,1)}, bf16[768,768]{1,0:T(8,128)(2,1)})) %all-reduce.3.cloned.1.call-update) | async-done | bytes 3538960 | tf_op jit(solution)/shard_map/psum | solution.py:110
  448.9 3.6 fusion.6
  452.5 0.6 fusion.8
  453.1 0.6 copy-done.4
  453.7 0.4 copy-done.5
  454.1 2.1 fusion.14
  456.2 5.1 %convolution_convert_fusion.3 = bf16[512,768]{1,0:T(8,128)(2,1)} fusion(bf16[768,768]{1,0:T(8,128)(2,1)} %get-tuple-element.12, bf16[1,768,768]{2,1,0:T(8,128)(2,1)S(1)} %copy-done.2, f32[768]{0:T(1024)S(1)} %get-tuple-element.21, f32[768]{0:T(1024)S(1)} %get-tuple-element.22, f32[512,768]{1,0:T(8,128)} %fusion.14, bf16[768,768]{1,0:T(8,128)(2,1)} %get-tuple-element.14, ...), kind=kOutput, calls=%fused_computation.44 | convolution fusion | flops 1218969600 | bytes 7878656 | tf_op jit(solution)/shard_map/dot_general | solution.py:66
  (17 shorter events, 0.1 us)
Async XLA Ops:
  7.2 9.9 %copy-start = (bf16[512,768]{1,0:T(8,128)(2,1)S(1)}, bf16[512,768]{1,0:T(8,128)(2,1)}, u32[]{:S(2)}) copy-start(bf16[512,768]{1,0:T(8,128)(2,1)} %param.8) | copy-start | bytes 2359300
  7.2 10.1 %copy-start.1 = (bf16[512,768]{1,0:T(8,128)(2,1)S(1)}, bf16[512,768]{1,0:T(8,128)(2,1)}, u32[]{:S(2)}) copy-start(bf16[512,768]{1,0:T(8,128)(2,1)} %param.7) | copy-start | bytes 2359300
  7.2 79.8 %all-gather.4.cloned.1.call-start = ((), (), s32[]{:S(2)}) async-start(), calls=%async_computation | async-start | bytes 1216512 | tf_op jit(solution)/shard_map/all_gather | solution.py:85
  7.9 149.3 %all-gather.8.cloned.1.call-start = ((), (), s32[]{:S(2)}) async-start(), calls=%async_computation.2 | async-start | bytes 1216512 | tf_op jit(solution)/shard_map/all_gather | solution.py:86
  8.7 218.8 %all-gather.6.cloned.1.call-start = ((), (), s32[]{:S(2)}) async-start(), calls=%async_computation.1 | async-start | bytes 1216512 | tf_op jit(solution)/shard_map/all_gather | solution.py:87
  10.1 13.9 %collective-permute-start.1 = (bf16[512,768]{0,1:T(8,128)(2,1)S(1)}, bf16[512,768]{0,1:T(8,128)(2,1)}, u32[]{:S(2)}, u32[]{:S(2)}) collective-permute-start(bf16[512,768]{0,1:T(8,128)(2,1)S(1)} %copy.14), channel_id=1, source_target_pairs={{0,16},{16,32},{32,48},{48,64},{64,80},{80,96},{96,112},{112,128},... | collective-permute-start | bytes 2359304 | tf_op jit(solution)/shard_map/ppermute | solution.py:15
  15.1 219.0 %collective-permute-start = (bf16[512,768]{1,0:T(8,128)(2,1)}, bf16[512,768]{1,0:T(8,128)(2,1)}, u32[]{:S(2)}, u32[]{:S(2)}) collective-permute-start(bf16[512,768]{1,0:T(8,128)(2,1)} %param.9), channel_id=1, source_target_pairs={{0,16},{16,32},{32,48},{48,64},{64,80},{80,96},{96,112},{112,128},... | collective-permute-start | bytes 2359304 | tf_op jit(solution)/shard_map/ppermute | solution.py:15
  17.0 431.8 %all-reduce.3.cloned.1.call-start = ((), (), s32[]{:S(2)}) async-start(), calls=%async_computation.3 | async-start | bytes 7077888 | tf_op jit(solution)/shard_map/psum | solution.py:110
  89.0 71.5 %copy-start.6 = (f32[512,1]{0,1:T(1,128)S(1)}, f32[512,1]{0,1:T(1,128)}, u32[]{:S(2)}) copy-start(f32[512,1]{0,1:T(1,128)} %param.10) | copy-start | bytes 6148
  159.3 1.2 copy-start.7
  229.8 2.1 copy-start.8
  448.9 3.7 copy-start.2
  448.9 3.7 copy-start.3
  452.5 1.3 copy-start.4
  452.5 1.6 copy-start.5
Sparse Core Ops, SparseCore 0:
  10.1 76.7 all-gather.3
  89.1 68.1 all-gather.7
  159.3 68.0 all-gather.5
  234.2 214.5 all-reduce.2
where the time goes:
time: 469 us; the launch traced here: 468 us
  waiting for transfers between devices  392 us (84%)
  matrix products  38.3 us (8%)
  between operations  14 us (3%)
  other arithmetic  10.3 us (2%)
  starting transfers between devices  7.02 us (1%)
  local copies, waits for them, and re-layouts  6.67 us (1%)
    psum x1, waiting for transfers between devices, body(): lax.psum(grad_down.astype(jnp.bfloat16), 'context').astype(jnp.float32)  204 us
    all_gather x1, waiting for transfers between devices, body(): lax.all_gather(w_up, 'context', axis=1, tiled=True)  68.2 us
    all_gather x1, waiting for transfers between devices, body(): lax.all_gather(w_down, 'context', axis=1, tiled=True)  63.7 us
    all_gather x1, waiting for transfers between devices, body(): lax.all_gather(w_gate, 'context', axis=1, tiled=True)  49.4 us
    sub x1, matrix products, window_block(): powers = jnp.exp(scores - row_max)  11 us
  transfers between devices with their start and end apart: 6, of which 5 were waited for; matrix products, arithmetic and copies ran while one was open for 9% of the time, Pallas kernels for 0%

commit v1 on v0

v1 whole, which is shorter than its diff:
```python
import functools
import math

import jax
import jax.numpy as jnp
from jax import lax
from jax.experimental import pallas as pl
from jax.experimental.pallas import tpu as pltpu
from jax.sharding import PartitionSpec as P

MESH = pl.DeviceIdType.MESH
F32 = jnp.float32
BF16 = jnp.bfloat16
HD = 128
WINDOW = 512
NZ = 16
TOK = 512
FD = 768
SLAB = FD // NZ
HALF = FD // 2
SENDS = ((8, 7), (7, 8), (8, 7))
NN = (((1,), (0,)), ((), ()))
NT = (((1,), (1,)), ((), ()))
TN = (((0,), (0,)), ((), ()))


def dot(a, b, dims):
    return lax.dot_general(a, b, dims, preferred_element_type=F32)


def kernel(
    q_in, k_in, v_in, step_ref, wg_ref, wu_ref, wd_ref, wout, fout,
    qs, kcat, vcat, fk, fq, tgt, wpad, wsib, w_all, grad, grad_sib, run, w_t, fresh, sq_mine, sq_sib, u_all, hid,
    in_sem, halo_send, halo_recv, pad_send, pad_recv, a_send, a_recv, ad_send, ad_recv,
    g_send, g_recv, r_send, r_recv, q_send, q_recv, u_send, u_recv, ud_send, ud_recv,
):
    c = lax.axis_index("context")
    core = lax.rem(c, 2)
    z = lax.div(c, 2)
    n = 2 * NZ
    sib = c + 1 - 2 * core
    nxt = (lax.rem(c + 2, n), lax.rem(c + n - 2, n))
    following = lax.rem(c + 1, n)

    def around(k):
        return lax.rem(z + k + 2 * NZ, NZ)

    def rows(slab):
        return pl.ds(pl.multiple_of(slab * SLAB, 16), SLAB)

    mine = pl.ds(pl.multiple_of(core * HALF, 128), HALF)
    other = pl.ds(pl.multiple_of((1 - core) * HALF, 128), HALF)

    def remote(src, dst, send, recv, to):
        return pltpu.make_async_remote_copy(
            src_ref=src, dst_ref=dst, send_sem=send, recv_sem=recv,
            device_id={"context": to}, device_id_type=MESH,
        )

    loads = (
        pltpu.make_async_copy(k_in, kcat.at[pl.ds(WINDOW, TOK)], in_sem.at[0]),
        pltpu.make_async_copy(v_in, vcat.at[pl.ds(WINDOW, TOK)], in_sem.at[1]),
        pltpu.make_async_copy(q_in, qs, in_sem.at[2]),
    )
    for load in loads:
        load.start()

    barrier = pltpu.get_barrier_semaphore()
    for step in (1, 2, n - 1, n - 2):
        pl.semaphore_signal(
            barrier, inc=1, device_id={"context": lax.rem(c + step, n)}, device_id_type=MESH
        )
    for m, ref in enumerate((wg_ref, wu_ref, wd_ref)):
        block = ref[0].astype(F32)
        wpad[m] = jnp.concatenate([block, jnp.zeros((8, FD), F32)], axis=0).astype(BF16)
    pl.semaphore_wait(barrier, 4)

    pad = remote(wpad, wsib, pad_send, pad_recv, sib)
    pad.start()
    pad.wait()
    for m in range(3):
        own = wpad[m].astype(F32)[:24]
        sibs = wsib[m].astype(F32)[:24]
        low = jnp.where(core == 0, own, sibs)
        high = jnp.where(core == 0, sibs, own)
        w_all[m, rows(z), :] = jnp.concatenate([low, high], axis=0).astype(BF16)

    def ring_gather(buf, z_send, z_recv, d_send, d_recv, filler):
        def z_copy(d, m, s):
            slab = around(-s) if d == 0 else around(s)
            view = buf.at[m, rows(slab), mine]
            return remote(view, view, z_send.at[d, m, s], z_recv.at[d, m, s], nxt[d])

        def d_copy(d, m, s):
            slab = around(-s) if d == 0 else around(s)
            view = buf.at[m, rows(slab), mine]
            return remote(view, view, d_send.at[d, m, s], d_recv.at[d, m, s], sib)

        for m in range(3):
            for d in range(2):
                z_copy(d, m, 0).start()
        filler(0)

        def turn(s, carry):
            for m in range(3):
                for d in range(2):
                    z_copy(d, m, s - 1).wait_recv()
                    z_copy(d, m, s).start()
                    d_copy(d, m, s).start()
            filler(s)
            return carry

        lax.fori_loop(1, 7, turn, 0)
        for m in range(3):
            for d in range(2):
                z_copy(d, m, 6).wait_recv()
                if SENDS[m][d] == 8:
                    z_copy(d, m, 7).start()
                d_copy(d, m, 7).start()
        for m in range(3):
            for d in range(2):
                if SENDS[m][d] == 8:
                    z_copy(d, m, 7).wait_recv()
                    d_copy(d, m, 8).start()

        def settle(s, carry):
            for m in range(3):
                for d in range(2):
                    z_copy(d, m, s - 1).wait_send()
                    d_copy(d, m, s).wait()
            return carry

        lax.fori_loop(1, 8, settle, 0)
        for m in range(3):
            for d in range(2):
                if SENDS[m][d] == 8:
                    z_copy(d, m, 7).wait_send()
                    d_copy(d, m, 8).wait()

    halo = (
        remote(kcat.at[pl.ds(WINDOW, TOK)], kcat.at[pl.ds(0, WINDOW)], halo_send.at[0], halo_recv.at[0], following),
        remote(vcat.at[pl.ds(WINDOW, TOK)], vcat.at[pl.ds(0, WINDOW)], halo_send.at[1], halo_recv.at[1], following),
    )

    def prepare(b):
        r = pl.ds(pl.multiple_of(b * 64, 64), 64)
        near = pl.ds(pl.multiple_of(b * 64 + WINDOW, 64), 64)
        k = kcat[near, :].astype(F32)
        fk[r, :] = (k * lax.rsqrt(jnp.mean(k * k, axis=-1, keepdims=True) + 1e-06)).astype(BF16)
        x = qs[r, :].astype(F32)
        fq[r, :] = (x * lax.rsqrt(jnp.mean(x * x, axis=-1, keepdims=True) + 1e-06)).astype(BF16)
        tgt[r, :] = (-(step_ref[r, :] * vcat[near, :].astype(F32))).astype(BF16)

    def gather_filler(s):
        if isinstance(s, int):
            for load in loads:
                load.wait()

            def body(b, carry):
                prepare(b)
                return carry

            lax.fori_loop(0, 8, body, 0)

    ring_gather(w_all, a_send, a_recv, ad_send, ad_recv, gather_filler)
    for copy in halo:
        copy.start()

    def hidden_block(b, carry):
        cols = pl.ds(pl.multiple_of(b * 256, 256), 256)
        gate = dot(fk[...], w_all[0, :, cols], NN)
        up = dot(fk[...], w_all[1, :, cols], NN)
        sg = jax.nn.sigmoid(gate)
        hidden = (gate * sg * up).astype(BF16)
        back = dot(tgt[...], w_all[2, cols, :], NT)
        d_gate = (back * up * sg * (1.0 + gate * (1.0 - sg))).astype(BF16)
        d_up = (back * gate * sg).astype(BF16)
        grad[0, cols, :] = dot(d_gate, fk[...], TN).astype(BF16)
        grad[1, cols, :] = dot(d_up, fk[...], TN).astype(BF16)
        grad[2, :, cols] = dot(tgt[...], hidden, TN).astype(BF16)
        return carry

    lax.fori_loop(0, 3, hidden_block, 0)

    def g_copy(m):
        return remote(grad.at[m, :, other], grad_sib.at[m], g_send.at[m], g_recv.at[m], sib)

    for m in range(3):
        g_copy(m).start()

    pick = (
        lax.broadcasted_iota(jnp.int32, (SLAB, FD), 1)
        == lax.broadcasted_iota(jnp.int32, (SLAB, FD), 0) + z * SLAB
    ).astype(BF16)
    for m in range(3):
        w_t[m] = dot(pick, w_all[m], NT)

    for m in range(3):
        g_copy(m).wait_recv()
    for copy in halo:
        copy.wait_recv()

    def local(m, slab):
        return grad[m, rows(slab), mine].astype(F32) + grad_sib[m, rows(slab), :].astype(F32)

    def r_copy(d, m, s):
        return remote(run.at[d, m, s], run.at[d, m, s + 1], r_send.at[d, m, s], r_recv.at[d, m, s], nxt[d])

    def r_slab(d, m, s):
        return around(SENDS[m][0] - s) if d == 0 else around(s - SENDS[m][1])

    low_limit = jnp.where(c == 0, WINDOW, 0)

    def attend(piece):
        h = lax.div(piece, 4)
        first = pl.multiple_of(lax.rem(piece, 4) * 128, 128)
        cols = pl.ds(pl.multiple_of(h * HD, HD), HD)
        kb = kcat[pl.ds(first, 640), cols]
        vb = vcat[pl.ds(first, 640), cols]
        scores = dot(qs[pl.ds(first, 128), cols], kb, NT) * (1.0 / math.sqrt(HD))
        t = lax.broadcasted_iota(jnp.int32, (128, 640), 0)
        j = lax.broadcasted_iota(jnp.int32, (128, 640), 1)
        allowed = (j > t) & (j <= t + WINDOW) & (j + first >= low_limit)
        scores = jnp.where(allowed, scores, -1e30)
        powers = jnp.exp(scores - jnp.max(scores, axis=-1, keepdims=True))
        total = jnp.sum(powers, axis=-1, keepdims=True)
        wout[pl.ds(first, 128), cols] = (dot(powers.astype(BF16), vb, NN) / total).astype(BF16)

    for m in range(3):
        for d in range(2):
            run[d, m, 0] = local(m, r_slab(d, m, 0)).astype(BF16)
            r_copy(d, m, 0).start()
        attend(m)

    def reduce_turn(s, carry):
        for m in range(3):
            for d in range(2):
                r_copy(d, m, s - 1).wait_recv()
                run[d, m, s] = (run[d, m, s].astype(F32) + local(m, r_slab(d, m, s))).astype(BF16)
                r_copy(d, m, s).start()
            attend(s * 3 + m)
        return carry

    lax.fori_loop(1, 7, reduce_turn, 0)
    for m in range(3):
        for d in range(2):
            if SENDS[m][d] == 8:
                r_copy(d, m, 6).wait_recv()
                run[d, m, 7] = (run[d, m, 7].astype(F32) + local(m, r_slab(d, m, 7))).astype(BF16)
                r_copy(d, m, 7).start()
        attend(21 + m)

    def q_copy(m):
        return remote(sq_mine.at[m], sq_sib.at[m], q_send.at[m], q_recv.at[m], sib)

    for m in range(3):
        total = local(m, z)
        for d in range(2):
            last = SENDS[m][d]
            r_copy(d, m, last - 1).wait_recv()
            total += run[d, m, last].astype(F32)
        new = w_t[m, :, mine] - total
        fresh[m] = new
        sq_mine[m] = jnp.broadcast_to(jnp.sum(new * new, axis=1, keepdims=True), (SLAB, 128))
        q_copy(m).start()
    for m in range(3):
        old = w_t[m]
        old_ms = jnp.mean(old * old, axis=1, keepdims=True)
        q_copy(m).wait()
        new_ms = (sq_mine[m, :, 0:1] + sq_sib[m, :, 0:1]) * (1.0 / FD)
        u_all[m, rows(z), mine] = (fresh[m] * (jnp.sqrt(old_ms) * lax.rsqrt(new_ms + 1e-06))).astype(BF16)

    def own_copy(m):
        view = u_all.at[m, rows(z), mine]
        return remote(view, view, ud_send.at[0, m, 0], ud_recv.at[0, m, 0], sib)

    for m in range(3):
        own_copy(m).start()

    ring_gather(u_all, u_send, u_recv, ud_send, ud_recv, lambda s: None)

    for m in range(3):
        own_copy(m).wait()

    def apply_block(b, carry):
        cols = pl.ds(pl.multiple_of(b * 256, 256), 256)
        gate = dot(fq[...], u_all[0, cols, :], NT)
        up = dot(fq[...], u_all[1, cols, :], NT)
        hid[:, cols] = (gate * jax.nn.sigmoid(gate) * up).astype(BF16)
        return carry

    lax.fori_loop(0, 3, apply_block, 0)

    def out_block(b, carry):
        cols = pl.ds(pl.multiple_of(b * 256, 256), 256)
        fout[:, cols] = dot(hid[...], u_all[2, cols, :], NT).astype(BF16)
        return carry

    lax.fori_loop(0, 3, out_block, 0)

    for m in range(3):
        g_copy(m).wait_send()
        for d in range(2):
            for s in range(SENDS[m][d]):
                r_copy(d, m, s).wait_send()
    for copy in halo:
        copy.wait_send()


def body(query_rows, key_rows, value_rows, step_sizes, w_gate, w_up, w_down):
    dma = pltpu.SemaphoreType.DMA
    vmem = pltpu.VMEM
    anywhere = pl.BlockSpec(memory_space=pl.ANY)
    inside = pl.BlockSpec(memory_space=pltpu.VMEM)
    return pl.pallas_call(
        kernel,
        out_shape=(jax.ShapeDtypeStruct((TOK, FD), BF16), jax.ShapeDtypeStruct((TOK, FD), BF16)),
        in_specs=[anywhere] * 3 + [inside] * 4,
        out_specs=(inside, inside),
        scratch_shapes=[
            vmem((TOK, FD), BF16),
            vmem((TOK + WINDOW, FD), BF16),
            vmem((TOK + WINDOW, FD), BF16),
            vmem((TOK, FD), BF16),
            vmem((TOK, FD), BF16),
            vmem((TOK, FD), BF16),
            vmem((3, 32, FD), BF16),
            vmem((3, 32, FD), BF16),
            vmem((3, FD, FD), BF16),
            vmem((3, FD, FD), BF16),
            vmem((3, FD, HALF), BF16),
            vmem((2, 3, 9, SLAB, HALF), BF16),
            vmem((3, SLAB, FD), F32),
            vmem((3, SLAB, HALF), F32),
            vmem((3, SLAB, 128), F32),
            vmem((3, SLAB, 128), F32),
            vmem((3, FD, FD), BF16),
            vmem((TOK, FD), BF16),
            dma((3,)), dma((2,)), dma((2,)), dma, dma,
            dma((2, 3, 8)), dma((2, 3, 8)), dma((2, 3, 9)), dma((2, 3, 9)),
            dma((3,)), dma((3,)), dma((2, 3, 8)), dma((2, 3, 8)), dma((3,)), dma((3,)),
            dma((2, 3, 8)), dma((2, 3, 8)), dma((2, 3, 9)), dma((2, 3, 9)),
        ],
        compiler_params=pltpu.CompilerParams(
            collective_id=0, has_side_effects=True, vmem_limit_bytes=56 * 2**20
        ),
        cost_estimate=pl.CostEstimate(flops=7 * 10**9, bytes_accessed=5 * 10**6, transcendentals=4 * 10**6),
        name="attend_and_update",
    )(query_rows, key_rows, value_rows, step_sizes, w_gate, w_up, w_down)


def solution(mesh):
    tokens = P(("seqs", "context"), "fheads")
    weights = P("fheads", "context", None)
    return jax.shard_map(
        body,
        mesh=mesh,
        in_specs=(tokens,) * 4 + (weights,) * 3,
        out_specs=(tokens, tokens),
        check_vma=False,
    )
```

time: 469 us -> 136 us (0.29)
  waiting for transfers between devices: 392 us -> 0 us
  Pallas kernels: 0 us -> 130 us
  matrix products: 38.3 us -> 0 us
  between operations: 14 us -> 0.65 us
  other arithmetic: 10.3 us -> 0 us
  starting transfers between devices: 7.02 us -> 0 us
    psum x1 -> x0, waiting for transfers between devices: 204 us -> none  [body(): lax.psum(grad_down.astype(jnp.bfloat16), 'context').astype(jnp.float32)]
    all_gather x3 -> x0, waiting for transfers between devices: 181 us -> none  [the longest x1 68.2 us: body(): lax.all_gather(w_up, 'context', axis=1, tiled=True)]
    pallas_call x0 -> x1, Pallas kernels: none -> 130 us  [body(): pl.pallas_call(kernel, out_shape=(jax.ShapeDtypeStruct((TOK, FD), BF16),...]
    dot_general x9 -> x0, matrix products: 27.3 us -> none  [the longest x3 7.51 us: dot_rows(): lax.dot_general(first_op, second_op, (((0,), (0,)), ((), ())), preferred_...]
    sub x1 -> x0, matrix products: 11 us -> none  [window_block(): powers = jnp.exp(scores - row_max)]
    ppermute x2 -> x0, starting transfers between devices: 6.86 us -> none  [passed_along(): return lax.ppermute(x, axis, pairs)]
  transfers between devices with their start and end apart: 6 -> 0, of which waited for: 5 -> 0; matrix products, arithmetic and copies ran while one was open for 9% -> 0% of each run, Pallas kernels for 0% -> 0%
where the time goes in v1:
time: 136 us
  Pallas kernels  130 us (96%)
  local copies, waits for them, and re-layouts  4.55 us (3%)
    pallas_call x1, Pallas kernels, body(): pl.pallas_call(kernel, out_shape=(jax.ShapeDtypeStruct((TOK, FD), BF16),...  130 us
    unnamed x5, local copies, waits for them, and re-layouts  4.55 us

profile of v1, /device:TPU:1, one launch (start us, length us, event | category | flops | bytes accessed | tf_op | source)
XLA Modules:
  0.0 135.6 jit_solution(4902017831472949574)
XLA Ops:
  0.6 1.5 %copy.9.step_ref = f32[512,1]{1,0:T(8,128)} copy(f32[512,1]{0,1:T(1,128)} %param.10) | data formatting | bytes 4096 | tf_op args[3]
  2.2 130.4 %attend_and_update.1 = (bf16[512,768]{1,0:T(8,128)(2,1)}, bf16[512,768]{1,0:T(8,128)(2,1)}) custom-call(bf16[512,768]{1,0:T(8,128)(2,1)} %q_in.1, bf16[512,768]{1,0:T(8,128)(2,1)} %k_in.1, bf16[512,768]{1,0:T(8,128)(2,1)} %v_in.1, f32[512,1]{1,0:T(8,128)} %copy.9.step_ref, bf16[1,24,768]{2,1,0:T(8,128)(2,1)} %wg_ref.1, bf16[1,24,768]{2,1,0:T(8,128)(2,1)} %wu_ref.1, ...), custom_call_target="tpu_custom_call" | custom-call | flops 7000000000 | bytes 5000000 | tf_op jit(solution)/shard_map/attend_and_update/pallas_call | solution.py:315
  132.6 0.0 copy-start
  132.6 2.1 %copy.12 = bf16[512,768]{1,0:T(8,128)(2,1)} copy(bf16[512,768]{1,0:T(8,128)(2,1)} %get-tuple-element.4) | data formatting | bytes 1572864
  134.7 0.0 copy-done
  134.7 0.9 copy.13
Async XLA Ops:
  132.6 2.1 %copy-start = (bf16[512,768]{1,0:T(8,128)(2,1)S(1)}, bf16[512,768]{1,0:T(8,128)(2,1)}, u32[]{:S(2)}) copy-start(bf16[512,768]{1,0:T(8,128)(2,1)} %get-tuple-element.5) | copy-start | bytes 2359300

commit v2 on v1

v2 whole, which is shorter than its diff:
```python
import functools
import math

import jax
import jax.numpy as jnp
from jax import lax
from jax.experimental import pallas as pl
from jax.experimental.pallas import tpu as pltpu
from jax.sharding import PartitionSpec as P

MESH = pl.DeviceIdType.MESH
F32 = jnp.float32
BF16 = jnp.bfloat16
HD = 128
WINDOW = 512
NZ = 16
TOK = 512
FD = 768
SLAB = FD // NZ
UNITS = 9
TOKENS = ((0, 2), (2, 2), (4, 2), (6, 2), (8, 1))
NN = (((1,), (0,)), ((), ()))
NT = (((1,), (1,)), ((), ()))
TN = (((0,), (0,)), ((), ()))


def dot(a, b, dims):
    return lax.dot_general(a, b, dims, preferred_element_type=F32)


def kernel(
    q_in, k_in, v_in, step_ref, wg_ref, wu_ref, wd_ref, wout, fout,
    qs, kcat, vcat, fk, fq, tgt, wpad, wsib, w_all, grad, grad_sib, run, w_t, last_mine, last_sib, u_all,
    hid, d_gate, d_up,
    in_sem, halo_send, halo_recv, pad_send, pad_recv, a_send, a_recv, ad_send, ad_recv,
    g_send, g_recv, r_send, r_recv, f_send, f_recv, u_send, u_recv, ud_send, ud_recv,
):
    c = lax.axis_index("context")
    core = lax.rem(c, 2)
    z = lax.div(c, 2)
    n = 2 * NZ
    sg = 1 - 2 * core
    sib = c + sg
    nxt = lax.rem(c + 2 * sg + n, n)
    following = lax.rem(c + 1, n)
    units = [pl.ds(3 * m, 3) for m in range(3)]
    tokens = [pl.ds(*t) for t in TOKENS]
    all_tokens = range(len(TOKENS))
    is_up = core == 0
    is_down = core == 1

    def around(k):
        return lax.rem(k + 2 * NZ, NZ)

    def remote(src, dst, send, recv, to):
        return pltpu.make_async_remote_copy(
            src_ref=src, dst_ref=dst, send_sem=send, recv_sem=recv, device_id=to, device_id_type=MESH
        )

    to_sib = {"context": sib}
    to_nxt = {"context": nxt}

    loads = (
        pltpu.make_async_copy(k_in, kcat.at[pl.ds(WINDOW, TOK)], in_sem.at[0]),
        pltpu.make_async_copy(v_in, vcat.at[pl.ds(WINDOW, TOK)], in_sem.at[1]),
        pltpu.make_async_copy(q_in, qs, in_sem.at[2]),
    )
    for load in loads:
        load.start()

    barrier = pltpu.get_barrier_semaphore()
    for step in (1, 2, n - 1, n - 2):
        pl.semaphore_signal(
            barrier, inc=1, device_id={"context": lax.rem(c + step, n)}, device_id_type=MESH
        )
    for m, ref in enumerate((wd_ref, wg_ref, wu_ref)):
        block = ref[0].astype(F32)
        wpad[m] = jnp.concatenate([block, jnp.zeros((8, FD), F32)], axis=0).astype(BF16)
    pl.semaphore_wait(barrier, 4)

    pad = remote(wpad, wsib, pad_send, pad_recv, to_sib)
    pad.start()
    pad.wait()
    for m in range(3):
        own = wpad[m].astype(F32)[:24]
        sibs = wsib[m].astype(F32)[:24]
        low = jnp.where(core == 0, own, sibs)
        high = jnp.where(core == 0, sibs, own)
        w_all[z, units[m]] = jnp.concatenate([low, high], axis=0).astype(BF16).reshape(3, 16, FD)

    def away(s):
        return around(z - sg * s)

    def ring(buf, z_send, z_recv, d_send, d_recv):
        def z_copy(t, s):
            view = buf.at[away(s), tokens[t]]
            return remote(view, view, z_send.at[t, s], z_recv.at[t, s], to_nxt)

        def d_copy(s):
            view = buf.at[away(s)]
            return remote(view, view, d_send.at[s], d_recv.at[s], to_sib)

        return z_copy, d_copy

    def pass_on(z_copy, d_copy, filler):
        def turn(s, carry):
            for t in all_tokens:
                z_copy(t, s - 1).wait_recv()
                z_copy(t, s).start()
            d_copy(s).start()
            filler(s)
            return carry

        lax.fori_loop(1, 7, turn, 0)
        for t in all_tokens:
            z_copy(t, 6).wait_recv()
            pl.when(is_up)(lambda: z_copy(t, 7).start())
        d_copy(7).start()

    def collect(z_copy, d_copy):
        @pl.when(is_up)
        def _():
            for t in all_tokens:
                z_copy(t, 7).wait_recv()
            d_copy(8).start()

        for s in range(1, 8):
            d_copy(s).wait_recv()
        pl.when(is_down)(lambda: d_copy(8).wait_recv())

    a_copy, ad_copy = ring(w_all, a_send, a_recv, ad_send, ad_recv)
    u_copy, ud_copy = ring(u_all, u_send, u_recv, ud_send, ud_recv)

    halo = (
        remote(kcat.at[pl.ds(WINDOW, TOK)], kcat.at[pl.ds(0, WINDOW)], halo_send.at[0], halo_recv.at[0], {"context": following}),
        remote(vcat.at[pl.ds(WINDOW, TOK)], vcat.at[pl.ds(0, WINDOW)], halo_send.at[1], halo_recv.at[1], {"context": following}),
    )

    for t in all_tokens:
        a_copy(t, 0).start()
    for load in loads:
        load.wait()

    def prepare(b, carry):
        r = pl.ds(pl.multiple_of(b * 64, 64), 64)
        near = pl.ds(pl.multiple_of(b * 64 + WINDOW, 64), 64)
        k = kcat[near, :].astype(F32)
        fk[r, :] = (k * lax.rsqrt(jnp.mean(k * k, axis=-1, keepdims=True) + 1e-06)).astype(BF16)
        x = qs[r, :].astype(F32)
        fq[r, :] = (x * lax.rsqrt(jnp.mean(x * x, axis=-1, keepdims=True) + 1e-06)).astype(BF16)
        return carry

    lax.fori_loop(0, 8, prepare, 0)
    for b in range(TOK // 128):
        step = jnp.transpose(jnp.broadcast_to(step_ref[b : b + 1, :], (128, 128)))[:, 0:1]
        near = pl.ds(b * 128 + WINDOW, 128)
        tgt[b * 128 : b * 128 + 128, :] = (-(step * vcat[near, :].astype(F32))).astype(BF16)

    pass_on(a_copy, ad_copy, lambda s: None)
    for copy in halo:
        copy.start()
    collect(a_copy, ad_copy)

    def whole(buf, m):
        return buf[:, units[m]].reshape(FD, FD)

    give = pl.ds(jnp.where(core == 0, 8, 1), 8)

    def g_copy(m):
        return remote(grad.at[give, units[m]], grad_sib.at[:, units[m]], g_send.at[m], g_recv.at[m], to_sib)

    def local(t, s):
        away_by = 8 - s
        theirs = jnp.where(core == 0, away_by - 1, 8 - away_by)
        return grad[around(sg * away_by), tokens[t]].astype(F32) + grad_sib[theirs, tokens[t]].astype(F32)

    def r_copy(t, s):
        return remote(run.at[s, tokens[t]], run.at[s + 1, tokens[t]], r_send.at[t, s], r_recv.at[t, s], to_nxt)

    def gradient(m, a, b):
        full = dot(a[...], b[...], TN).astype(BF16).reshape(NZ, 3, 16, FD)
        for k in range(NZ):
            grad[around(k - z), units[m]] = full[k]
        g_copy(m).start()

    def begin(first, last):
        for s, here in ((0, is_up), (1, is_down)):

            @pl.when(here)
            def _():
                for t in range(first, last):
                    run[s, tokens[t]] = local(t, s).astype(BF16)
                    r_copy(t, s).start()

    gate = dot(fk[...], whole(w_all, 1), NN)
    up = dot(fk[...], whole(w_all, 2), NN)
    sg_gate = jax.nn.sigmoid(gate)
    hid[...] = (gate * sg_gate * up).astype(BF16)
    gradient(0, tgt, hid)
    back = dot(tgt[...], whole(w_all, 0), NT)
    d_gate[...] = (back * up * sg_gate * (1.0 + gate * (1.0 - sg_gate))).astype(BF16)
    d_up[...] = (back * gate * sg_gate).astype(BF16)
    g_copy(0).wait_recv()
    begin(0, 1)
    gradient(1, d_gate, fk)
    gradient(2, d_up, fk)
    g_copy(1).wait_recv()
    begin(1, 2)
    g_copy(2).wait_recv()
    begin(2, 5)

    pick = (
        lax.broadcasted_iota(jnp.int32, (SLAB, FD), 1)
        == lax.broadcasted_iota(jnp.int32, (SLAB, FD), 0) + z * SLAB
    ).astype(BF16)
    for m in range(3):
        w_t[m] = dot(pick, whole(w_all, m), NT)

    def reduce_step(t, s):
        r_copy(t, s - 1).wait_recv()
        run[s, tokens[t]] = (run[s, tokens[t]].astype(F32) + local(t, s)).astype(BF16)
        r_copy(t, s).start()

    @pl.when(is_up)
    def _():
        for t in all_tokens:
            reduce_step(t, 1)

    def reduce_turn(s, carry):
        for t in all_tokens:
            reduce_step(t, s)
        return carry

    lax.fori_loop(2, 8, reduce_turn, 0)

    def f_copy(m):
        return remote(last_mine.at[units[m]], last_sib.at[units[m]], f_send.at[m], f_recv.at[m], to_sib)

    for m, ready in enumerate(((0, 1), (2,), (3, 4))):
        for t in ready:
            r_copy(t, 7).wait_recv()
        last_mine[units[m]] = (run[8, units[m]].astype(F32) + grad[0, units[m]].astype(F32)).astype(BF16)
        f_copy(m).start()

    for m, ready in enumerate(((0,), (1, 2), (3, 4))):
        old = w_t[m]
        old_ms = jnp.mean(old * old, axis=1, keepdims=True)
        f_copy(m).wait_recv()
        total = last_mine[units[m]].astype(F32) + last_sib[units[m]].astype(F32)
        new = old - total.reshape(SLAB, FD)
        new_ms = jnp.mean(new * new, axis=1, keepdims=True)
        u_all[z, units[m]] = (new * (jnp.sqrt(old_ms) * lax.rsqrt(new_ms + 1e-06))).astype(BF16).reshape(3, 16, FD)
        for t in ready:
            u_copy(t, 0).start()

    for copy in halo:
        copy.wait_recv()
    low_limit = jnp.where(c == 0, WINDOW, 0)

    def attend(piece):
        h = lax.div(piece, 4)
        first = pl.multiple_of(lax.rem(piece, 4) * 128, 128)
        cols = pl.ds(pl.multiple_of(h * HD, HD), HD)
        kb = kcat[pl.ds(first, 640), cols]
        vb = vcat[pl.ds(first, 640), cols]
        scores = dot(qs[pl.ds(first, 128), cols], kb, NT) * (1.0 / math.sqrt(HD))
        t = lax.broadcasted_iota(jnp.int32, (128, 640), 0)
        j = lax.broadcasted_iota(jnp.int32, (128, 640), 1)
        allowed = (j > t) & (j <= t + WINDOW) & (j + first >= low_limit)
        scores = jnp.where(allowed, scores, -1e30)
        powers = jnp.exp(scores - jnp.max(scores, axis=-1, keepdims=True))
        total = jnp.sum(powers, axis=-1, keepdims=True)
        wout[pl.ds(first, 128), cols] = (dot(powers.astype(BF16), vb, NN) / total).astype(BF16)

    def attend_some(s):
        for k in range(3):
            attend(3 * s + k)

    attend_some(0)
    pass_on(u_copy, ud_copy, attend_some)
    attend_some(7)
    collect(u_copy, ud_copy)

    gate = dot(fq[...], whole(u_all, 1), NT)
    up = dot(fq[...], whole(u_all, 2), NT)
    hid[...] = (gate * jax.nn.sigmoid(gate) * up).astype(BF16)
    fout[...] = dot(hid[...], whole(u_all, 0), NT).astype(BF16)

    def sent(s, carry):
        ad_copy(s + 1).wait_send()
        ud_copy(s + 1).wait_send()
        for t in all_tokens:
            a_copy(t, s).wait_send()
            r_copy(t, s + 1).wait_send()
            u_copy(t, s).wait_send()
        return carry

    lax.fori_loop(0, 7, sent, 0)

    @pl.when(is_up)
    def _():
        ad_copy(8).wait_send()
        ud_copy(8).wait_send()
        for t in all_tokens:
            a_copy(t, 7).wait_send()
            r_copy(t, 0).wait_send()
            u_copy(t, 7).wait_send()

    for m in range(3):
        g_copy(m).wait_send()
        f_copy(m).wait_send()
    for copy in halo:
        copy.wait_send()


def body(query_rows, key_rows, value_rows, step_sizes, w_gate, w_up, w_down):
    dma = pltpu.SemaphoreType.DMA
    vmem = pltpu.VMEM
    anywhere = pl.BlockSpec(memory_space=pl.ANY)
    inside = pl.BlockSpec(memory_space=pltpu.VMEM)
    slabs = (NZ, UNITS, 16, FD)
    return pl.pallas_call(
        kernel,
        out_shape=(jax.ShapeDtypeStruct((TOK, FD), BF16), jax.ShapeDtypeStruct((TOK, FD), BF16)),
        in_specs=[anywhere] * 3 + [inside] * 4,
        out_specs=(inside, inside),
        scratch_shapes=[
            vmem((TOK, FD), BF16),
            vmem((TOK + WINDOW, FD), BF16),
            vmem((TOK + WINDOW, FD), BF16),
            vmem((TOK, FD), BF16),
            vmem((TOK, FD), BF16),
            vmem((TOK, FD), BF16),
            vmem((3, 32, FD), BF16),
            vmem((3, 32, FD), BF16),
            vmem(slabs, BF16),
            vmem(slabs, BF16),
            vmem((8, UNITS, 16, FD), BF16),
            vmem((9, UNITS, 16, FD), BF16),
            vmem((3, SLAB, FD), F32),
            vmem((UNITS, 16, FD), BF16),
            vmem((UNITS, 16, FD), BF16),
            vmem(slabs, BF16),
            vmem((TOK, FD), BF16),
            vmem((TOK, FD), BF16),
            vmem((TOK, FD), BF16),
            dma((3,)), dma((2,)), dma((2,)), dma, dma,
            dma((5, 8)), dma((5, 8)), dma((9,)), dma((9,)),
            dma((3,)), dma((3,)), dma((5, 8)), dma((5, 8)), dma((3,)), dma((3,)),
            dma((5, 8)), dma((5, 8)), dma((9,)), dma((9,)),
        ],
        compiler_params=pltpu.CompilerParams(
            collective_id=0, has_side_effects=True, vmem_limit_bytes=56 * 2**20
        ),
        cost_estimate=pl.CostEstimate(flops=7 * 10**9, bytes_accessed=5 * 10**6, transcendentals=4 * 10**6),
        name="attend_and_update",
    )(query_rows, key_rows, value_rows, step_sizes.reshape(TOK // 128, 128), w_gate, w_up, w_down)


def solution(mesh):
    tokens = P(("seqs", "context"), "fheads")
    weights = P("fheads", "context", None)
    return jax.shard_map(
        body,
        mesh=mesh,
        in_specs=(tokens,) * 4 + (weights,) * 3,
        out_specs=(tokens, tokens),
        check_vma=False,
    )
```

time: 136 us -> 121 us (0.89)
  Pallas kernels: 130 us -> 117 us
  local copies, waits for them, and re-layouts: 4.55 us -> 3.02 us
    pallas_call x1, Pallas kernels: 130 us -> 117 us  [body(): pl.pallas_call(kernel, out_shape=(jax.ShapeDtypeStruct((TOK, FD), BF16),...]
    unnamed x5 -> x4, local copies, waits for them, and re-layouts: 4.55 us -> 3.02 us
where the time goes in v2:
time: 121 us
  Pallas kernels  117 us (97%)
  local copies, waits for them, and re-layouts  3.02 us (2%)
    pallas_call x1, Pallas kernels, body(): pl.pallas_call(kernel, out_shape=(jax.ShapeDtypeStruct((TOK, FD), BF16),...  117 us
    unnamed x4, local copies, waits for them, and re-layouts  3.02 us

profile of v2, /device:TPU:1, one launch (start us, length us, event | category | flops | bytes accessed | tf_op | source)
XLA Modules:
  0.0 120.5 jit_solution(6393715001709992918)
XLA Ops:
  0.6 116.9 %attend_and_update.1 = (bf16[512,768]{1,0:T(8,128)(2,1)}, bf16[512,768]{1,0:T(8,128)(2,1)}) custom-call(bf16[512,768]{1,0:T(8,128)(2,1)} %q_in.1, bf16[512,768]{1,0:T(8,128)(2,1)} %k_in.1, bf16[512,768]{1,0:T(8,128)(2,1)} %v_in.1, f32[4,128]{1,0:T(4,128)} %bitcast.1, bf16[1,24,768]{2,1,0:T(8,128)(2,1)} %wg_ref.1, bf16[1,24,768]{2,1,0:T(8,128)(2,1)} %wu_ref.1, ...), custom_call_target="tpu_custom_call" | custom-call | flops 7000000000 | bytes 5000000 | tf_op jit(solution)/shard_map/attend_and_update/pallas_call | solution.py:322
  117.5 0.0 copy-start
  117.5 2.1 %copy.11 = bf16[512,768]{1,0:T(8,128)(2,1)} copy(bf16[512,768]{1,0:T(8,128)(2,1)} %get-tuple-element.4) | data formatting | bytes 1572864
  119.7 0.0 copy-done
  119.7 0.9 copy.12
Async XLA Ops:
  117.5 2.1 %copy-start = (bf16[512,768]{1,0:T(8,128)(2,1)S(1)}, bf16[512,768]{1,0:T(8,128)(2,1)}, u32[]{:S(2)}) copy-start(bf16[512,768]{1,0:T(8,128)(2,1)} %get-tuple-element.5) | copy-start | bytes 2359300

commit v3 on v2

--- a/solution.py
+++ b/solution.py
@@ -19,6 +19,7 @@
 SLAB = FD // NZ
 UNITS = 9
 TOKENS = ((0, 2), (2, 2), (4, 2), (6, 2), (8, 1))
+FIRST_OF = {0: 0, 1: 1, 3: 2}
 NN = (((1,), (0,)), ((), ()))
 NT = (((1,), (1,)), ((), ()))
 TN = (((0,), (0,)), ((), ()))
@@ -29,7 +30,7 @@
 
 
 def kernel(
-    q_in, k_in, v_in, step_ref, wg_ref, wu_ref, wd_ref, wout, fout,
+    q_in, k_in, v_in, step_ref, wg_ref, wu_ref, wd_ref, out,
     qs, kcat, vcat, fk, fq, tgt, wpad, wsib, w_all, grad, grad_sib, run, w_t, last_mine, last_sib, u_all,
     hid, d_gate, d_up,
     in_sem, halo_send, halo_recv, pad_send, pad_recv, a_send, a_recv, ad_send, ad_recv,
@@ -39,15 +40,15 @@
     core = lax.rem(c, 2)
     z = lax.div(c, 2)
     n = 2 * NZ
-    sg = 1 - 2 * core
-    sib = c + sg
+    sg = 2 * core - 1
+    sib = c - sg
     nxt = lax.rem(c + 2 * sg + n, n)
     following = lax.rem(c + 1, n)
     units = [pl.ds(3 * m, 3) for m in range(3)]
     tokens = [pl.ds(*t) for t in TOKENS]
     all_tokens = range(len(TOKENS))
-    is_up = core == 0
-    is_down = core == 1
+    is_far = core == 0
+    is_near = core == 1
 
     def around(k):
         return lax.rem(k + 2 * NZ, NZ)
@@ -114,11 +115,11 @@
         lax.fori_loop(1, 7, turn, 0)
         for t in all_tokens:
             z_copy(t, 6).wait_recv()
-            pl.when(is_up)(lambda: z_copy(t, 7).start())
+            pl.when(is_far)(lambda: z_copy(t, 7).start())
         d_copy(7).start()
 
     def collect(z_copy, d_copy):
-        @pl.when(is_up)
+        @pl.when(is_far)
         def _():
             for t in all_tokens:
                 z_copy(t, 7).wait_recv()
@@ -126,7 +127,7 @@
 
         for s in range(1, 8):
             d_copy(s).wait_recv()
-        pl.when(is_down)(lambda: d_copy(8).wait_recv())
+        pl.when(is_near)(lambda: d_copy(8).wait_recv())
 
     a_copy, ad_copy = ring(w_all, a_send, a_recv, ad_send, ad_recv)
     u_copy, ud_copy = ring(u_all, u_send, u_recv, ud_send, ud_recv)
@@ -164,15 +165,14 @@
     def whole(buf, m):
         return buf[:, units[m]].reshape(FD, FD)
 
-    give = pl.ds(jnp.where(core == 0, 8, 1), 8)
-
-    def g_copy(m):
-        return remote(grad.at[give, units[m]], grad_sib.at[:, units[m]], g_send.at[m], g_recv.at[m], to_sib)
+    def g_copy(m, s):
+        return remote(
+            grad.at[around(sg * (s - 8)), units[m]], grad_sib.at[s, units[m]],
+            g_send.at[m, s], g_recv.at[m, s], to_sib,
+        )
 
     def local(t, s):
-        away_by = 8 - s
-        theirs = jnp.where(core == 0, away_by - 1, 8 - away_by)
-        return grad[around(sg * away_by), tokens[t]].astype(F32) + grad_sib[theirs, tokens[t]].astype(F32)
+        return grad[around(sg * (8 - s)), tokens[t]].astype(F32) + grad_sib[s, tokens[t]].astype(F32)
 
     def r_copy(t, s):
         return remote(run.at[s, tokens[t]], run.at[s + 1, tokens[t]], r_send.at[t, s], r_recv.at[t, s], to_nxt)
@@ -181,14 +181,18 @@
         full = dot(a[...], b[...], TN).astype(BF16).reshape(NZ, 3, 16, FD)
         for k in range(NZ):
             grad[around(k - z), units[m]] = full[k]
-        g_copy(m).start()
+        pl.when(is_near)(lambda: g_copy(m, 0).start())
+        for s in range(1, 8):
+            g_copy(m, s).start()
 
     def begin(first, last):
-        for s, here in ((0, is_up), (1, is_down)):
+        for s, here in ((0, is_far), (1, is_near)):
 
             @pl.when(here)
             def _():
                 for t in range(first, last):
+                    if t in FIRST_OF:
+                        g_copy(FIRST_OF[t], s).wait_recv()
                     run[s, tokens[t]] = local(t, s).astype(BF16)
                     r_copy(t, s).start()
 
@@ -200,14 +204,10 @@
     back = dot(tgt[...], whole(w_all, 0), NT)
     d_gate[...] = (back * up * sg_gate * (1.0 + gate * (1.0 - sg_gate))).astype(BF16)
     d_up[...] = (back * gate * sg_gate).astype(BF16)
-    g_copy(0).wait_recv()
     begin(0, 1)
     gradient(1, d_gate, fk)
     gradient(2, d_up, fk)
-    g_copy(1).wait_recv()
-    begin(1, 2)
-    g_copy(2).wait_recv()
-    begin(2, 5)
+    begin(1, 5)
 
     pick = (
         lax.broadcasted_iota(jnp.int32, (SLAB, FD), 1)
@@ -218,10 +218,12 @@
 
     def reduce_step(t, s):
         r_copy(t, s - 1).wait_recv()
+        if t in FIRST_OF:
+            g_copy(FIRST_OF[t], s).wait_recv()
         run[s, tokens[t]] = (run[s, tokens[t]].astype(F32) + local(t, s)).astype(BF16)
         r_copy(t, s).start()
 
-    @pl.when(is_up)
+    @pl.when(is_far)
     def _():
         for t in all_tokens:
             reduce_step(t, 1)
@@ -270,7 +272,7 @@
         scores = jnp.where(allowed, scores, -1e30)
         powers = jnp.exp(scores - jnp.max(scores, axis=-1, keepdims=True))
         total = jnp.sum(powers, axis=-1, keepdims=True)
-        wout[pl.ds(first, 128), cols] = (dot(powers.astype(BF16), vb, NN) / total).astype(BF16)
+        out[0, pl.ds(first, 128), cols] = (dot(powers.astype(BF16), vb, NN) / total).astype(BF16)
 
     def attend_some(s):
         for k in range(3):
@@ -284,7 +286,7 @@
     gate = dot(fq[...], whole(u_all, 1), NT)
     up = dot(fq[...], whole(u_all, 2), NT)
     hid[...] = (gate * jax.nn.sigmoid(gate) * up).astype(BF16)
-    fout[...] = dot(hid[...], whole(u_all, 0), NT).astype(BF16)
+    out[1] = dot(hid[...], whole(u_all, 0), NT).astype(BF16)
 
     def sent(s, carry):
         ad_copy(s + 1).wait_send()
@@ -297,7 +299,7 @@
 
     lax.fori_loop(0, 7, sent, 0)
 
-    @pl.when(is_up)
+    @pl.when(is_far)
     def _():
         ad_copy(8).wait_send()
         ud_copy(8).wait_send()
@@ -307,7 +309,9 @@
             u_copy(t, 7).wait_send()
 
     for m in range(3):
-        g_copy(m).wait_send()
+        pl.when(is_near)(lambda: g_copy(m, 0).wait_send())
+        for s in range(1, 8):
+            g_copy(m, s).wait_send()
         f_copy(m).wait_send()
     for copy in halo:
         copy.wait_send()
@@ -319,11 +323,11 @@
     anywhere = pl.BlockSpec(memory_space=pl.ANY)
     inside = pl.BlockSpec(memory_space=pltpu.VMEM)
     slabs = (NZ, UNITS, 16, FD)
-    return pl.pallas_call(
+    out = pl.pallas_call(
         kernel,
-        out_shape=(jax.ShapeDtypeStruct((TOK, FD), BF16), jax.ShapeDtypeStruct((TOK, FD), BF16)),
+        out_shape=jax.ShapeDtypeStruct((2, TOK, FD), BF16),
         in_specs=[anywhere] * 3 + [inside] * 4,
-        out_specs=(inside, inside),
+        out_specs=inside,
         scratch_shapes=[
             vmem((TOK, FD), BF16),
             vmem((TOK + WINDOW, FD), BF16),
@@ -346,7 +350,7 @@
             vmem((TOK, FD), BF16),
             dma((3,)), dma((2,)), dma((2,)), dma, dma,
             dma((5, 8)), dma((5, 8)), dma((9,)), dma((9,)),
-            dma((3,)), dma((3,)), dma((5, 8)), dma((5, 8)), dma((3,)), dma((3,)),
+            dma((3, 8)), dma((3, 8)), dma((5, 8)), dma((5, 8)), dma((3,)), dma((3,)),
             dma((5, 8)), dma((5, 8)), dma((9,)), dma((9,)),
         ],
         compiler_params=pltpu.CompilerParams(
@@ -355,6 +359,7 @@
         cost_estimate=pl.CostEstimate(flops=7 * 10**9, bytes_accessed=5 * 10**6, transcendentals=4 * 10**6),
         name="attend_and_update",
     )(query_rows, key_rows, value_rows, step_sizes.reshape(TOK // 128, 128), w_gate, w_up, w_down)
+    return out[0], out[1]
 
 
 def solution(mesh):

time: 121 us -> 114 us (0.942)
  Pallas kernels: 117 us -> 111 us
    pallas_call x1, Pallas kernels: 117 us -> 111 us  [body(): pl.pallas_call(kernel, out_shape=jax.ShapeDtypeStruct((2, TOK, FD), BF16)...]
    unnamed x4 -> x0, local copies, waits for them, and re-layouts: 3.02 us -> none
    squeeze x0 -> x1, local copies, waits for them, and re-layouts: none -> 2.61 us  [body(): return (out[0], out[1])]
where the time goes in v3:
time: 114 us
  Pallas kernels  111 us (97%)
  local copies, waits for them, and re-layouts  2.61 us (2%)
    pallas_call x1, Pallas kernels, body(): pl.pallas_call(kernel, out_shape=jax.ShapeDtypeStruct((2, TOK, FD), BF16)...  111 us
    squeeze x1, local copies, waits for them, and re-layouts, body(): return (out[0], out[1])  2.61 us

profile of v3, /device:TPU:1, one launch (start us, length us, event | category | flops | bytes accessed | tf_op | source)
XLA Modules:
  0.0 113.9 jit_solution(4384548451782479829)
XLA Ops:
  0.6 110.7 %attend_and_update.1 = bf16[2,512,768]{2,1,0:T(8,128)(2,1)} custom-call(bf16[512,768]{1,0:T(8,128)(2,1)} %q_in.1, bf16[512,768]{1,0:T(8,128)(2,1)} %k_in.1, bf16[512,768]{1,0:T(8,128)(2,1)} %v_in.1, f32[4,128]{1,0:T(4,128)} %bitcast.5, bf16[1,24,768]{2,1,0:T(8,128)(2,1)} %wg_ref.1, bf16[1,24,768]{2,1,0:T(8,128)(2,1)} %wu_ref.1, bf16[1,24,768]{2,1,0:T(8,128)(2,1)} %wd_ref.1), custom_call_target="tpu_custom_call" | custom-call | flops 7000000000 | bytes 5000000 | tf_op jit(solution)/shard_map/attend_and_update/pallas_call | solution.py:326
  111.3 2.6 %slice_bitcast_fusion = (bf16[512,768]{1,0:T(8,128)(2,1)}, bf16[512,768]{1,0:T(8,128)(2,1)}) fusion(bf16[2,512,768]{2,1,0:T(8,128)(2,1)} %attend_and_update.1), kind=kLoop, calls=%fused_computation | loop fusion | bytes 3145728 | tf_op jit(solution)/shard_map/squeeze | solution.py:362

commit v4 on v3

--- a/solution.py
+++ b/solution.py
@@ -157,9 +157,8 @@
         near = pl.ds(b * 128 + WINDOW, 128)
         tgt[b * 128 : b * 128 + 128, :] = (-(step * vcat[near, :].astype(F32))).astype(BF16)
 
-    pass_on(a_copy, ad_copy, lambda s: None)
-    for copy in halo:
-        copy.start()
+    pass_on(a_copy, ad_copy, lambda s: pl.when(s == 5)(halo[0].start))
+    halo[1].start()
     collect(a_copy, ad_copy)
 
     def whole(buf, m):

time: 114 us -> 115 us (level)
  no operation moved by 1% of the time
where the time goes in v4:
time: 115 us
  Pallas kernels  111 us (97%)
  local copies, waits for them, and re-layouts  2.61 us (2%)
    pallas_call x1, Pallas kernels, body(): pl.pallas_call(kernel, out_shape=jax.ShapeDtypeStruct((2, TOK, FD), BF16)...  111 us
    squeeze x1, local copies, waits for them, and re-layouts, body(): return (out[0], out[1])  2.61 us

profile of v4, /device:TPU:1, one launch (start us, length us, event | category | flops | bytes accessed | tf_op | source)
XLA Modules:
  0.0 114.7 jit_solution(840086093579455422)
XLA Ops:
  0.6 111.5 %attend_and_update.1 = bf16[2,512,768]{2,1,0:T(8,128)(2,1)} custom-call(bf16[512,768]{1,0:T(8,128)(2,1)} %q_in.1, bf16[512,768]{1,0:T(8,128)(2,1)} %k_in.1, bf16[512,768]{1,0:T(8,128)(2,1)} %v_in.1, f32[4,128]{1,0:T(4,128)} %bitcast.5, bf16[1,24,768]{2,1,0:T(8,128)(2,1)} %wg_ref.1, bf16[1,24,768]{2,1,0:T(8,128)(2,1)} %wu_ref.1, bf16[1,24,768]{2,1,0:T(8,128)(2,1)} %wd_ref.1), custom_call_target="tpu_custom_call" | custom-call | flops 7000000000 | bytes 5000000 | tf_op jit(solution)/shard_map/attend_and_update/pallas_call | solution.py:325
  112.1 2.6 %slice_bitcast_fusion = (bf16[512,768]{1,0:T(8,128)(2,1)}, bf16[512,768]{1,0:T(8,128)(2,1)}) fusion(bf16[2,512,768]{2,1,0:T(8,128)(2,1)} %attend_and_update.1), kind=kLoop, calls=%fused_computation | loop fusion | bytes 3145728 | tf_op jit(solution)/shard_map/squeeze | solution.py:361

commit v5 on v3

--- a/solution.py
+++ b/solution.py
@@ -97,9 +97,10 @@
             view = buf.at[away(s), tokens[t]]
             return remote(view, view, z_send.at[t, s], z_recv.at[t, s], to_nxt)
 
-        def d_copy(s):
-            view = buf.at[away(s)]
-            return remote(view, view, d_send.at[s], d_recv.at[s], to_sib)
+        def d_copy(s, t=None):
+            view = buf.at[away(s)] if t is None else buf.at[away(s), tokens[t]]
+            slot = s if t is None else s + t
+            return remote(view, view, d_send.at[slot], d_recv.at[slot], to_sib)
 
         return z_copy, d_copy
 
@@ -123,11 +124,15 @@
         def _():
             for t in all_tokens:
                 z_copy(t, 7).wait_recv()
-            d_copy(8).start()
+                d_copy(8, t).start()
 
         for s in range(1, 8):
             d_copy(s).wait_recv()
-        pl.when(is_near)(lambda: d_copy(8).wait_recv())
+
+        @pl.when(is_near)
+        def _():
+            for t in all_tokens:
+                d_copy(8, t).wait_recv()
 
     a_copy, ad_copy = ring(w_all, a_send, a_recv, ad_send, ad_recv)
     u_copy, ud_copy = ring(u_all, u_send, u_recv, ud_send, ud_recv)
@@ -301,9 +306,9 @@
 
     @pl.when(is_far)
     def _():
-        ad_copy(8).wait_send()
-        ud_copy(8).wait_send()
-        for t in all_tokens:
+        for t in all_tokens:
+            ad_copy(8, t).wait_send()
+            ud_copy(8, t).wait_send()
             a_copy(t, 7).wait_send()
             r_copy(t, 0).wait_send()
             u_copy(t, 7).wait_send()
@@ -349,9 +354,9 @@
             vmem((TOK, FD), BF16),
             vmem((TOK, FD), BF16),
             dma((3,)), dma((2,)), dma((2,)), dma, dma,
-            dma((5, 8)), dma((5, 8)), dma((9,)), dma((9,)),
+            dma((5, 8)), dma((5, 8)), dma((13,)), dma((13,)),
             dma((3, 8)), dma((3, 8)), dma((5, 8)), dma((5, 8)), dma((3,)), dma((3,)),
-            dma((5, 8)), dma((5, 8)), dma((9,)), dma((9,)),
+            dma((5, 8)), dma((5, 8)), dma((13,)), dma((13,)),
         ],
         compiler_params=pltpu.CompilerParams(
             collective_id=0, has_side_effects=True, vmem_limit_bytes=56 * 2**20

time: 114 us -> 114 us (level)
  no operation moved by 1% of the time
where the time goes in v5:
time: 114 us; the launch traced here: 113 us
  Pallas kernels  110 us (96%)
  local copies, waits for them, and re-layouts  2.61 us (2%)
    pallas_call x1, Pallas kernels, body(): pl.pallas_call(kernel, out_shape=jax.ShapeDtypeStruct((2, TOK, FD), BF16)...  110 us
    squeeze x1, local copies, waits for them, and re-layouts, body(): return (out[0], out[1])  2.61 us

profile of v5, /device:TPU:1, one launch (start us, length us, event | category | flops | bytes accessed | tf_op | source)
XLA Modules:
  0.0 113.5 jit_solution(15825068809408821633)
XLA Ops:
  0.6 110.2 %attend_and_update.1 = bf16[2,512,768]{2,1,0:T(8,128)(2,1)} custom-call(bf16[512,768]{1,0:T(8,128)(2,1)} %q_in.1, bf16[512,768]{1,0:T(8,128)(2,1)} %k_in.1, bf16[512,768]{1,0:T(8,128)(2,1)} %v_in.1, f32[4,128]{1,0:T(4,128)} %bitcast.5, bf16[1,24,768]{2,1,0:T(8,128)(2,1)} %wg_ref.1, bf16[1,24,768]{2,1,0:T(8,128)(2,1)} %wu_ref.1, bf16[1,24,768]{2,1,0:T(8,128)(2,1)} %wd_ref.1), custom_call_target="tpu_custom_call" | custom-call | flops 7000000000 | bytes 5000000 | tf_op jit(solution)/shard_map/attend_and_update/pallas_call | solution.py:331
  110.9 2.6 %slice_bitcast_fusion = (bf16[512,768]{1,0:T(8,128)(2,1)}, bf16[512,768]{1,0:T(8,128)(2,1)}) fusion(bf16[2,512,768]{2,1,0:T(8,128)(2,1)} %attend_and_update.1), kind=kLoop, calls=%fused_computation | loop fusion | bytes 3145728 | tf_op jit(solution)/shard_map/squeeze | solution.py:367
